TPU v7x, 256 devices: a whole 4x4x8 slice. The times are simulated.
256 devices in a mesh: row: 16 (over z_hi, y, core), col: 16 (over x, z_lo).
Axes of the slice: x: 4, y: 4, z: 8 (z_hi: 2, z_lo: 4; z = z_hi * 4 + z_lo), core: 2. Of those that a mesh axis runs over, the one named last changes fastest.
Arguments:
- slab_points: bfloat16 [64, 16384], P(None, ('row', 'col')), may hold values from -6 to 6
- col_points: bfloat16 [64, 262144], P(None, 'col'), may hold values from -6 to 6
- probes: bfloat16 [64, 262144], P(None, 'col'), may hold values from -6 to 6
Outputs:
- basis: bfloat16 [64, 16384], P(None, ('row', 'col'))
- image: float32 [64, 262144], P(None, ('col', 'row'))
All inputs are finite; a program needn't handle non-finite values.
Results may differ from a plain program's by a relative error of at most 0.0052.
Values may be sent and summed in bfloat16 or wider, within the bound.
A program may use at most 128 MiB of HBM per device.

v0:
```python
import math

import jax
import jax.numpy as jnp
from jax import lax
from jax.sharding import PartitionSpec as P


def body(slab_points, col_points, probes):
    slab_whole = lax.all_gather(slab_points, "col", axis=1, tiled=True)
    dims = slab_whole.shape[0]
    slab_count = slab_whole.shape[1]
    col_count = col_points.shape[1]
    width = math.gcd(col_count, 2048)
    blocks = col_count // width
    slab_total = slab_count * lax.axis_size("row")
    point_total = col_count * lax.axis_size("col")
    share = slab_count // lax.axis_size("col")
    slab_norm = jnp.sum(slab_whole.astype(jnp.float32) ** 2, axis=0)
    col_norm = jnp.sum(col_points.astype(jnp.float32) ** 2, axis=0)

    def make_tile(start):
        cols = lax.dynamic_slice_in_dim(col_points, start, width, 1)
        norms = lax.dynamic_slice_in_dim(col_norm, start, width, 0)
        inner = lax.dot_general(
            slab_whole, cols, (((0,), (0,)), ((), ())), preferred_element_type=jnp.float32
        )
        distance = slab_norm[:, None] + norms[None, :] - 2.0 * inner
        return jnp.exp(-8.0 * distance / dims).astype(jnp.bfloat16)

    def sample_step(total, which):
        start = which * width
        kernel = make_tile(start)
        probe_block = lax.dynamic_slice_in_dim(probes, start, width, 1)
        total = total + lax.dot_general(
            probe_block, kernel, (((1,), (1,)), ((), ())), preferred_element_type=jnp.float32
        )
        return (total, None)

    empty = jnp.zeros((probes.shape[0], slab_count), jnp.float32)
    partial_value, stored = lax.scan(sample_step, empty, jnp.arange(blocks, dtype=jnp.int32))
    sample = lax.psum(partial_value, "col")
    gram = lax.psum(jnp.dot(sample, sample.T, precision=lax.Precision.HIGHEST), "row") / slab_total
    lower = jnp.linalg.cholesky(gram)
    basis_full = jax.scipy.linalg.solve_triangular(lower, sample, lower=True).astype(jnp.bfloat16)
    basis_own = lax.dynamic_slice_in_dim(basis_full, lax.axis_index("col") * share, share, 1)

    def image_step(which, result):
        start = which * width
        kernel = make_tile(start)
        block_out = jnp.dot(basis_full, kernel, preferred_element_type=jnp.float32)
        return lax.dynamic_update_slice_in_dim(result, block_out, start, 1)

    terms = lax.fori_loop(
        0, blocks, image_step, jnp.zeros((probes.shape[0], col_count), jnp.float32)
    )
    image_scale = (
        jnp.sqrt(jnp.float32(probes.shape[0] * point_total) / jnp.trace(gram)) / slab_total
    )
    image = lax.psum_scatter(terms, "row", scatter_dimension=1, tiled=True) * image_scale
    return (basis_own, image)


def solution(mesh):
    return jax.shard_map(
        body,
        mesh=mesh,
        in_specs=(P(None, ("row", "col")), P(None, "col"), P(None, "col")),
        out_specs=(P(None, ("row", "col")), P(None, ("col", "row"))),
        check_vma=False,
    )
```

profile of v0, /device:TPU:9, one launch (start us, length us, event | category | flops | bytes accessed | tf_op | source)
XLA Modules:
  0.0 501.8 jit_solution(372806711789975218)
XLA Ops:
  7.2 0.8 copy.6
  8.0 38.4 %all_gather.3 = bf16[64,1024]{0,1:T(8,128)(2,1)S(1)} all-gather(bf16[64,64]{0,1:T(8,128)(2,1)S(1)} %copy.6), channel_id=1, replica_groups=mesh['row'=16,'col'=16] {'col'}, dimensions={1}, use_global_device_ids=true | all-gather | bytes 139264 | tf_op jit(solution)/shard_map/all_gather | solution.py:10
  46.8 2.1 multiply_reduce_fusion
  48.9 42.8 %while.29 = (s32[]{:T(128)}, f32[64,1024]{1,0:T(8,128)S(1)}, s32[8]{0:T(128)S(1)}, bf16[64,16384]{1,0:T(8,128)(2,1)}, f32[1024]{0:T(1024)S(1)}, /*index=5*/f32[1...) while((s32[]{:T(128)}, f32[64,1024]{1,0:T(8,128)S(1)}, ...), condition=%wide.region_3.4_spmd.clone, body=%wide.region_2.3_spmd.clone.sunk | while | flops 547487744 | bytes 1210044 | solution.py:41
  50.2 4.1 fusion.47
  55.5 4.0 fusion.47
  60.8 4.1 fusion.47
  66.2 4.1 fusion.47
  71.5 4.1 fusion.47
  76.9 4.1 fusion.47
  82.2 4.1 fusion.47
  87.6 4.1 fusion.47
  91.7 0.7 copy-done
  92.4 155.1 %all-reduce.2.cloned.1.call-done = f32[64,1024]{1,0:T(8,128)} async-done(((f32[64,1024]{1,0:T(8,128)}), f32[64,1024]{1,0:T(8,128)}) %all-reduce.2.cloned.1.call-update) | async-done | bytes 262160 | tf_op jit(solution)/shard_map/psum | solution.py:42
  247.5 1.4 fusion.25
  248.9 78.8 %psum.15 = f32[64,64]{1,0:T(8,128)S(1)} all-reduce(f32[64,64]{1,0:T(8,128)S(1)} %fusion.25), channel_id=1, replica_groups=mesh['row'=16,'col'=16] {'row'}, use_global_device_ids=true, to_apply=%region_5.6 | all-reduce | flops 4096 | bytes 32768 | tf_op jit(solution)/shard_map/psum | solution.py:43
  328.4 5.8 %cholesky.17 = f32[64,64]{1,0:T(8,128)S(1)} custom-call(f32[64,64]{1,0:T(8,128)S(1)} %get-tuple-element.354), custom_call_target="Cholesky" | custom-call | tf_op jit(solution)/shard_map/jit(cholesky)/cholesky | solution.py:44
  334.3 0.7 compare_reduce_fusion
  335.6 4.9 custom-call.7
  340.5 1.4 convolution_convert_fusion
  341.9 2.3 broadcast_in_dim.19
  344.2 35.2 %while.28 = (s32[]{:T(128)}, f32[64,16384]{1,0:T(8,128)}, f32[1024]{0:T(1024)S(1)}, f32[16384]{0:T(1024)S(1)}, bf16[64,16384]{1,0:T(8,128)(2,1)}, /*index=5*/bf1...) while((s32[]{:T(128)}, f32[64,16384]{1,0:T(8,128)}, ...), condition=%wide.region_9.10_spmd, body=%wide.region_8.9_spmd.sunk | while | flops 547356672 | bytes 1078431 | solution.py:54
  344.2 4.4 fusion.43
  348.6 4.4 fusion.43
  353.0 4.4 fusion.43
  357.3 4.4 fusion.43
  361.7 4.4 fusion.43
  366.1 4.4 fusion.43
  370.5 4.4 fusion.43
  374.9 4.4 fusion.43
  380.8 112.5 %reduce-scatter.2.cloned.1.call-done = f32[64,1024]{1,0:T(8,128)} async-done(((f32[64,16384]{1,0:T(8,128)}), f32[64,1024]{1,0:T(8,128)}) %reduce-scatter.2.cloned.1.call-update) | async-done | bytes 262160 | tf_op jit(solution)/shard_map/reduce_scatter | solution.py:60
  493.3 1.7 broadcast_multiply_fusion
  (39 shorter events, 7.3 us)
Async XLA Ops:
  7.2 240.4 %all-reduce.2.cloned.1.call-start = ((), (), s32[]{:S(2)}) async-start(), calls=%async_computation.1 | async-start | bytes 524288 | tf_op jit(solution)/shard_map/psum | solution.py:42
  91.6 0.7 copy-start
  92.4 401.0 %reduce-scatter.2.cloned.1.call-start = ((), (), s32[]{:S(2)}) async-start(), calls=%async_computation.2 | async-start | bytes 4456448 | tf_op jit(solution)/shard_map/reduce_scatter | solution.py:60
Sparse Core Ops, SparseCore 0:
  92.5 154.9 all-reduce.1
  379.5 113.8 reduce-scatter.1
where the time goes:
time: 505 us; the launch traced here: 502 us
  waiting for transfers between devices  268 us (53%)
  blocking collectives  117 us (23%)
  matrix products  70.4 us (14%)
  other arithmetic  16.7 us (3%)
  between operations  14.9 us (3%)
  local copies, waits for them, and re-layouts  9.43 us (2%)
  loops' own time  5.54 us (1%)
    psum x1, waiting for transfers between devices, body(): sample = lax.psum(partial_value, 'col')  155 us
    reduce_scatter x1, waiting for transfers between devices, body(): lax.psum_scatter(terms, 'row', scatter_dimension=1, tiled=True)  113 us
    psum x1, blocking collectives, body(): lax.psum(jnp.dot(sample, sample.T, precision=lax.Precision.HIGHEST), 'row')  78.8 us
    all_gather x1, blocking collectives, body(): slab_whole = lax.all_gather(slab_points, 'col', axis=1, tiled=True)  38.4 us
    dot_general x8, matrix products, image_step(): block_out = jnp.dot(basis_full, kernel, preferred_element_type=jnp.float32)  35.2 us
    dot_general x8, matrix products, sample_step(): lax.dot_general(probe_block, kernel, (((1,), (1,)), ((), ())), preferred_...  32.5 us
  transfers between devices with their start and end apart: 2, of which 2 were waited for; matrix products, arithmetic and copies ran while one was open for 0% of the time, Pallas kernels for 0%

commit v1 on v0

v1 whole, which is shorter than its diff:
```python
import functools
import math

import jax
import jax.numpy as jnp
from jax import lax
from jax.experimental import pallas as pl
from jax.experimental.pallas import tpu as pltpu
from jax.sharding import PartitionSpec as P

F32 = jnp.float32
BF16 = jnp.bfloat16
MESH = pl.DeviceIdType.MESH
NN = (((1,), (0,)), ((), ()))
NT = (((1,), (1,)), ((), ()))
LOG2E = 1.4426950408889634
HIGHEST = lax.Precision.HIGHEST

NX, NZ, NY, NCORE = 4, 8, 4, 2
GROUP = NX * NZ
PEERS = NY * NCORE
DIMS = 64
PROBES = 64
BLK = 64
CHUNKS = 4
CA = 512
A = CHUNKS * CA
B = 8192
TB = 4096
OWN = 1024


def split3(v):
    h = v.astype(BF16).astype(F32)
    m = (v - h).astype(BF16).astype(F32)
    return h, m, v - h - m


def main_kernel(
    slab_ref, col_ref, probe_ref,
    zsum_ref, gsum_ref, sown_ref,
    cols, probes, yt, xall, xaug, kmat, spart, rsrecv, sfull, st,
    zsend, zmine, zcrecv, zyrecv, gsend, grecv, xown,
    in_sem, xs_sem, xr_sem, rs_s, rs_r, ag_s, ag_r, zc_s, zc_r, zy_s, zy_r, g_s, g_r,
):
    row = lax.axis_index("row")
    col = lax.axis_index("col")
    core = row % 2
    y = (row // 2) % 4
    z = (row // 8) * 4 + col % 4
    x = col // 4
    zhi = row // 8
    me = z * NX + x
    mine = y * NCORE + core
    my_chunk = (x - z + 8) % 4

    def group_id(g):
        gx = g % NX
        gz = g // NX
        return ((gz // 4) * 8 + y * 2 + core, gx * 4 + gz % 4)

    def peer_id(q):
        return (zhi * 8 + q, col)

    def owner(c, j):
        return j * NX + (c + j) % NX

    cp_c = pltpu.make_async_copy(col_ref.at[:, pl.ds(pl.multiple_of(zhi * B, B), B)], cols, in_sem.at[0])
    cp_p = pltpu.make_async_copy(
        probe_ref.at[:, pl.ds(pl.multiple_of(zhi * B, B), B)], probes.at[pl.ds(0, PROBES), :], in_sem.at[1]
    )
    cp_c.start()
    cp_p.start()

    barrier = pltpu.get_barrier_semaphore()

    def greet_group(r, _):
        pl.semaphore_signal(barrier, inc=1, device_id=group_id((me + r) % GROUP), device_id_type=MESH)
        return 0

    def greet_peer(r, _):
        pl.semaphore_signal(barrier, inc=1, device_id=peer_id((mine + r) % PEERS), device_id_type=MESH)
        return 0

    lax.fori_loop(1, GROUP, greet_group, 0)
    lax.fori_loop(1, PEERS, greet_peer, 0)

    s_in = slab_ref[...].astype(F32)
    packed = jnp.concatenate([s_in[: DIMS // 2], s_in[DIMS // 2 :]], axis=1).astype(BF16)
    xown[...] = packed
    xall[me] = packed
    probes[PROBES:, :] = jnp.zeros((128 - PROBES, B), BF16)

    pl.semaphore_wait(barrier, GROUP - 1 + PEERS - 1)

    def slab_copy(r):
        return pltpu.make_async_remote_copy(
            src_ref=xown,
            dst_ref=xall.at[me],
            send_sem=xs_sem.at[r - 1],
            recv_sem=xr_sem.at[me],
            device_id=group_id((me + r) % GROUP),
            device_id_type=MESH,
        )

    def slab_send(r, _):
        slab_copy(r).start()
        return 0

    lax.fori_loop(1, GROUP, slab_send, 0)

    cp_c.wait()
    alpha = LOG2E * 8.0 / DIMS

    def make_yt(i, _):
        b0 = pl.multiple_of(i * 512, 512)
        yv = cols[:, pl.ds(b0, 512)].astype(F32)
        yp = yv * (2.0 * alpha)
        h, m, l = split3(yp)
        nh, nm, nl = split3(-alpha * jnp.sum(yv * yv, axis=0, keepdims=True))
        r = lax.broadcasted_iota(jnp.int32, (DIMS, 512), 0)
        extra = jnp.where(
            r < 3, 1.0, jnp.where(r == 3, nh, jnp.where(r == 4, nm, jnp.where(r == 5, nl, 0.0)))
        )
        yt[pl.ds(b0, 512), 0:128] = jnp.transpose(jnp.concatenate([h, m], axis=0)).astype(BF16)
        yt[pl.ds(b0, 512), 128:256] = jnp.transpose(jnp.concatenate([l, extra], axis=0)).astype(BF16)
        return 0

    lax.fori_loop(0, B // 512, make_yt, 0)
    cp_p.wait()

    lane = lax.broadcasted_iota(jnp.int32, (DIMS // 2, 128), 1)

    def build_x(c):
        def wait_block(j, _):
            g = owner(c, j)

            @pl.when(g != me)
            def _():
                pltpu.make_async_remote_copy(
                    src_ref=xown, dst_ref=xall.at[g], send_sem=xs_sem.at[0], recv_sem=xr_sem.at[g],
                    device_id=group_id((me + 1) % GROUP), device_id_type=MESH,
                ).wait_recv()

            return 0

        lax.fori_loop(0, NZ, wait_block, 0)
        for pair in range(NZ // 2):
            va = xall[owner(c, 2 * pair)].astype(F32)
            vb = xall[owner(c, 2 * pair + 1)].astype(F32)
            even = jnp.where(lane < 64, va, pltpu.roll(vb, 64, 1))
            odd = jnp.where(lane < 64, pltpu.roll(va, 64, 1), vb)
            xv = jnp.concatenate([even, odd], axis=0)
            nh, nm, nl = split3(-alpha * jnp.sum(xv * xv, axis=0, keepdims=True))
            r = lax.broadcasted_iota(jnp.int32, (DIMS, 128), 0)
            extra = jnp.where(
                r == 0, nh,
                jnp.where(r == 1, nm, jnp.where(r == 2, nl, jnp.where(r < 6, 1.0, 0.0))),
            )
            whole = jnp.concatenate([xv, xv, xv, extra], axis=0).astype(BF16)
            xaug[:, pair * 128 : (pair + 1) * 128] = whole

    def rs_copy(c, j):
        g = owner(c, j)
        return pltpu.make_async_remote_copy(
            src_ref=spart.at[c, pl.ds(pl.multiple_of(j * 8, 8), 8), :],
            dst_ref=rsrecv.at[(me - g + GROUP) % GROUP - 1],
            send_sem=rs_s.at[c * NZ + j],
            recv_sem=rs_r.at[(me - g + GROUP) % GROUP - 1],
            device_id=group_id(g),
            device_id_type=MESH,
        )

    def ag_copy(r):
        rows = pl.ds(pl.multiple_of(z * 8, 8), 8)
        return pltpu.make_async_remote_copy(
            src_ref=sfull.at[my_chunk, rows, :],
            dst_ref=sfull.at[my_chunk, rows, :],
            send_sem=ag_s.at[r - 1],
            recv_sem=ag_r.at[my_chunk * NZ + z],
            device_id=group_id((me + r) % GROUP),
            device_id_type=MESH,
        )

    def reduce_own(c):
        @pl.when(my_chunk == c)
        def _():
            rows = pl.ds(pl.multiple_of(z * 8, 8), 8)

            def add(i, total):
                pltpu.make_async_remote_copy(
                    src_ref=rsrecv.at[i], dst_ref=rsrecv.at[i], send_sem=rs_s.at[0], recv_sem=rs_r.at[i],
                    device_id=group_id((me + 1) % GROUP), device_id_type=MESH,
                ).wait_recv()
                return total + rsrecv[i]

            sfull[c, rows, :] = lax.fori_loop(0, GROUP - 1, add, spart[c, rows, :])

            def send(r, _):
                ag_copy(r).start()
                return 0

            lax.fori_loop(1, GROUP, send, 0)

    def phase1(c, _):
        build_x(c)

        def tile(i, total):
            b0 = pl.multiple_of(i * TB, TB)
            t = lax.dot_general(yt[pl.ds(b0, TB), :], xaug[...], NN, preferred_element_type=F32)
            k = jnp.exp2(t).astype(BF16)
            kmat[pl.ds(b0, TB), pl.ds(pl.multiple_of(c * CA, CA), CA)] = k
            return total + lax.dot_general(
                probes[:, pl.ds(b0, TB)], k, NN, preferred_element_type=F32
            )[:PROBES]

        spart[c] = lax.fori_loop(0, B // TB, tile, jnp.zeros((PROBES, CA), F32))

        def send(j, _):
            @pl.when(owner(c, j) != me)
            def _():
                rs_copy(c, j).start()

            return 0

        lax.fori_loop(0, NZ, send, 0)

        @pl.when(c > 0)
        def _():
            reduce_own(c - 1)

        return 0

    lax.fori_loop(0, CHUNKS, phase1, 0)
    reduce_own(CHUNKS - 1)

    gsend[...] = jnp.zeros((PROBES, 128), F32)

    def take_chunk(c, g):
        def wait_piece(j, _):
            @pl.when(owner(c, j) != me)
            def _():
                rows = pl.ds(pl.multiple_of(j * 8, 8), 8)
                pltpu.make_async_remote_copy(
                    src_ref=sfull.at[c, rows, :], dst_ref=sfull.at[c, rows, :],
                    send_sem=ag_s.at[0], recv_sem=ag_r.at[c * NZ + j],
                    device_id=group_id((me + 1) % GROUP), device_id_type=MESH,
                ).wait_recv()

            return 0

        lax.fori_loop(0, NZ, wait_piece, 0)
        s = sfull[c]
        hi = s.astype(BF16).astype(F32)
        st[pl.ds(pl.multiple_of(c * CA, CA), CA), :] = jnp.transpose(
            jnp.concatenate([hi, s - hi], axis=0)
        ).astype(BF16)
        return g + lax.dot_general(s, s, NT, precision=HIGHEST, preferred_element_type=F32)

    gsend[:, 0:PROBES] = lax.fori_loop(0, CHUNKS, take_chunk, jnp.zeros((PROBES, PROBES), F32))

    def g_copy(r):
        return pltpu.make_async_remote_copy(
            src_ref=gsend, dst_ref=grecv.at[r - 1], send_sem=g_s.at[r - 1], recv_sem=g_r.at[r - 1],
            device_id=peer_id((mine + r) % PEERS), device_id_type=MESH,
        )

    def g_start(r, _):
        g_copy(r).start()
        return 0

    lax.fori_loop(1, PEERS, g_start, 0)

    wide = lax.broadcasted_iota(jnp.int32, (OWN // 2, 128), 1)

    def image_part(o):
        zt = lax.dot_general(
            kmat[pl.ds(pl.multiple_of(o * OWN, OWN), OWN), :], st[...], NN, preferred_element_type=F32
        )
        u = zt + pltpu.roll(zt, 64, 1)
        return jnp.where(wide < 64, u[: OWN // 2], u[OWN // 2 :])

    def zc_copy(t):
        return pltpu.make_async_remote_copy(
            src_ref=zsend.at[t], dst_ref=zcrecv.at[t], send_sem=zc_s.at[t], recv_sem=zc_r.at[t],
            device_id=peer_id(y * 2 + 1 - core), device_id_type=MESH,
        )

    def zy_copy(t):
        return pltpu.make_async_remote_copy(
            src_ref=zmine.at[t], dst_ref=zyrecv.at[t], send_sem=zy_s.at[t], recv_sem=zy_r.at[t],
            device_id=peer_id(((y + 1 + t) % NY) * 2 + core), device_id_type=MESH,
        )

    def phase2(t, _):
        yo = (y + 1 + t) % NY
        zsend[t] = image_part(yo * 2 + 1 - core)
        zc_copy(t).start()
        own = image_part(yo * 2 + core)
        zc_copy(t).wait_recv()
        zmine[t] = own + zcrecv[t]

        @pl.when(t < NY - 1)
        def _():
            zy_copy(t).start()

        return 0

    lax.fori_loop(0, NY, phase2, 0)

    def g_wait(r, total):
        g_copy(r).wait()
        return total + grecv[r - 1]

    gsum_ref[...] = lax.fori_loop(1, PEERS, g_wait, gsend[...])
    tile = sfull[my_chunk, :, pl.ds(pl.multiple_of((z // 2) * 128, 128), 128)]
    sown_ref[...] = jnp.where(z % 2 == 1, pltpu.roll(tile, 64, 1), tile)

    def xs_wait(r, _):
        slab_copy(r).wait_send()
        ag_copy(r).wait_send()
        return 0

    lax.fori_loop(1, GROUP, xs_wait, 0)

    def rs_wait(i, _):
        c = i // NZ
        j = i % NZ

        @pl.when(owner(c, j) != me)
        def _():
            rs_copy(c, j).wait_send()

        return 0

    lax.fori_loop(0, CHUNKS * NZ, rs_wait, 0)

    def zc_wait(t, _):
        zc_copy(t).wait_send()
        return 0

    lax.fori_loop(0, NY, zc_wait, 0)

    def zy_wait(t, total):
        zy_copy(t).wait()
        return total + zyrecv[t]

    zsum_ref[...] = lax.fori_loop(0, NY - 1, zy_wait, zmine[NY - 1])


def final_kernel(zsum_ref, gsum_ref, sown_ref, basis_ref, image_ref, *, slab_total, point_total):
    lane = lax.broadcasted_iota(jnp.int32, (PROBES, 128), 1)
    rows = lax.broadcasted_iota(jnp.int32, (PROBES, 128), 0)
    gram = gsum_ref[...] / slab_total
    diag = jnp.where(lane == rows, gram, 0.0)
    trace = jnp.sum(diag)
    m = jnp.where(lane < 64, gram, jnp.where(lane - 64 == rows, 1.0, 0.0))
    for k in range(PROBES - 1):
        pivot = m[k : k + 1, :]
        factor = m[:, k : k + 1] / m[k : k + 1, k : k + 1]
        m = m - jnp.where(rows > k, factor * pivot, 0.0)
    d = jnp.sum(jnp.where(lane == rows, m, 0.0), axis=1, keepdims=True)
    upper = jnp.where(lane >= 64, m / jnp.sqrt(d), 0.0)
    lower = pltpu.roll(upper, 64, 1)
    basis = lax.dot_general(
        lower[:, :64], sown_ref[...], NN, precision=HIGHEST, preferred_element_type=F32
    )
    basis_ref[...] = basis[:, :64].astype(BF16)
    scale = jnp.sqrt(jnp.float32(PROBES * point_total) / jnp.full((1, 1), trace)) / slab_total
    zs = zsum_ref[...]
    for half, w in ((0, lower), (1, upper)):
        image_ref[:, half * 512 : half * 512 + 512] = scale * lax.dot_general(
            w, zs, NT, precision=HIGHEST, preferred_element_type=F32
        )


def body(slab_points, col_points, probes):
    vmem = pl.BlockSpec(memory_space=pltpu.VMEM)
    dma = pltpu.SemaphoreType.DMA
    zsum, gsum, sown = pl.pallas_call(
        main_kernel,
        out_shape=(
            jax.ShapeDtypeStruct((OWN // 2, 128), F32),
            jax.ShapeDtypeStruct((PROBES, 128), F32),
            jax.ShapeDtypeStruct((PROBES, 128), F32),
        ),
        in_specs=[vmem, pl.BlockSpec(memory_space=pl.ANY), pl.BlockSpec(memory_space=pl.ANY)],
        out_specs=(vmem, vmem, vmem),
        scratch_shapes=[
            pltpu.VMEM((DIMS, B), BF16),
            pltpu.VMEM((128, B), BF16),
            pltpu.VMEM((B, 256), BF16),
            pltpu.VMEM((GROUP, 32, 128), BF16),
            pltpu.VMEM((256, CA), BF16),
            pltpu.VMEM((B, A), BF16),
            pltpu.VMEM((CHUNKS, PROBES, CA), F32),
            pltpu.VMEM((GROUP - 1, 8, CA), F32),
            pltpu.VMEM((CHUNKS, PROBES, CA), F32),
            pltpu.VMEM((A, 128), BF16),
            pltpu.VMEM((NY, OWN // 2, 128), F32),
            pltpu.VMEM((NY, OWN // 2, 128), F32),
            pltpu.VMEM((NY, OWN // 2, 128), F32),
            pltpu.VMEM((NY - 1, OWN // 2, 128), F32),
            pltpu.VMEM((PROBES, 128), F32),
            pltpu.VMEM((PEERS - 1, PROBES, 128), F32),
            pltpu.VMEM((32, 128), BF16),
            dma((2,)),
            dma((GROUP - 1,)),
            dma((GROUP,)),
            dma((CHUNKS * NZ,)),
            dma((GROUP - 1,)),
            dma((GROUP - 1,)),
            dma((CHUNKS * NZ,)),
            dma((NY,)),
            dma((NY,)),
            dma((NY - 1,)),
            dma((NY - 1,)),
            dma((PEERS - 1,)),
            dma((PEERS - 1,)),
        ],
        compiler_params=pltpu.CompilerParams(
            collective_id=0, has_side_effects=True, vmem_limit_bytes=62 << 20
        ),
        name="slab_kernel",
    )(slab_points, col_points, probes)
    return pl.pallas_call(
        functools.partial(final_kernel, slab_total=16384, point_total=262144),
        out_shape=(
            jax.ShapeDtypeStruct((PROBES, BLK), BF16),
            jax.ShapeDtypeStruct((PROBES, OWN), F32),
        ),
        in_specs=[vmem, vmem, vmem],
        out_specs=(vmem, vmem),
        name="factor_and_image",
    )(zsum, gsum, sown)


def solution(mesh):
    return jax.shard_map(
        body,
        mesh=mesh,
        in_specs=(P(None, ("row", "col")), P(None, "col"), P(None, "col")),
        out_specs=(P(None, ("row", "col")), P(None, ("col", "row"))),
        check_vma=False,
    )
```

time: 505 us -> 91.2 us (0.18)
  waiting for transfers between devices: 268 us -> 0 us
  blocking collectives: 117 us -> 0 us
  Pallas kernels: 0 us -> 90.3 us
  matrix products: 70.4 us -> 0 us
  other arithmetic: 16.7 us -> 0 us
  between operations: 14.9 us -> 0.64 us
  local copies, waits for them, and re-layouts: 9.43 us -> 0 us
  loops' own time: 5.54 us -> 0 us
    psum x1 -> x0, waiting for transfers between devices: 155 us -> none  [body(): sample = lax.psum(partial_value, 'col')]
    reduce_scatter x1 -> x0, waiting for transfers between devices: 113 us -> none  [body(): lax.psum_scatter(terms, 'row', scatter_dimension=1, tiled=True)]
    pallas_call x0 -> x2, Pallas kernels: none -> 90.3 us  [the longest x1 82.6 us: body(): pl.pallas_call(main_kernel, out_shape=(jax.ShapeDtypeStruct((OWN // 2, 12...]
    psum x1 -> x0, blocking collectives: 78.8 us -> none  [body(): lax.psum(jnp.dot(sample, sample.T, precision=lax.Precision.HIGHEST), 'row')]
    dot_general x17 -> x0, matrix products: 69 us -> none  [the longest x8 35.2 us: image_step(): block_out = jnp.dot(basis_full, kernel, preferred_element_type=jnp.float32)]
    all_gather x1 -> x0, blocking collectives: 38.4 us -> none  [body(): slab_whole = lax.all_gather(slab_points, 'col', axis=1, tiled=True)]
    another operation x5 -> x0, other arithmetic: 12.1 us -> none  [the longest x3 6.58 us: body(): lower = jnp.linalg.cholesky(gram)]
    another operation x2 -> x0, loops' own time: 5.54 us -> none  [the longest x1 5.54 us: body(): lax.scan(sample_step, empty, jnp.arange(blocks, dtype=jnp.int32))]
  transfers between devices with their start and end apart: 2 -> 0, of which waited for: 2 -> 0; matrix products, arithmetic and copies ran while one was open for 0% -> 0% of each run, Pallas kernels for 0% -> 0%
where the time goes in v1:
time: 91.2 us; the launch traced here: 91 us
  Pallas kernels  90.3 us (99%)
    pallas_call x1, Pallas kernels, body(): pl.pallas_call(main_kernel, out_shape=(jax.ShapeDtypeStruct((OWN // 2, 12...  82.6 us
    pallas_call x1, Pallas kernels, body(): pl.pallas_call(functools.partial(final_kernel, slab_total=16384, point_to...  7.69 us

profile of v1, /device:TPU:9, one launch (start us, length us, event | category | flops | bytes accessed | tf_op | source)
XLA Modules:
  0.0 91.0 jit_solution(11364985313535779976)
XLA Ops:
  0.6 82.6 %slab_kernel.1 = (f32[512,128]{1,0:T(8,128)}, f32[64,128]{1,0:T(8,128)}, f32[64,128]{1,0:T(8,128)}) custom-call(bf16[64,64]{1,0:T(8,128)(2,1)} %slab_ref.1, bf16[64,16384]{1,0:T(8,128)(2,1)} %col_ref.1, bf16[64,16384]{1,0:T(8,128)(2,1)} %probe_ref.1), custom_call_target="tpu_custom_call" | custom-call | tf_op jit(solution)/shard_map/slab_kernel/pallas_call | solution.py:380
  83.3 7.7 %factor_and_image.1 = (bf16[64,64]{1,0:T(8,128)(2,1)}, f32[64,1024]{1,0:T(8,128)}) custom-call(f32[512,128]{1,0:T(8,128)} %get-tuple-element.5.zsum_ref, f32[64,128]{1,0:T(8,128)} %get-tuple-element.6.gsum_ref, f32[64,128]{1,0:T(8,128)} %get-tuple-element.7.sown_ref), custom_call_target="tpu_custom_call" | custom-call | tf_op jit(solution)/shard_map/factor_and_image/pallas_call | solution.py:426

commit v2 on v0

v2 whole, which is shorter than its diff:
```python
import functools
import math

import jax
import jax.numpy as jnp
from jax import lax
from jax.experimental import pallas as pl
from jax.experimental.pallas import tpu as pltpu
from jax.sharding import PartitionSpec as P

F32 = jnp.float32
BF16 = jnp.bfloat16
MESH = pl.DeviceIdType.MESH
NN = (((1,), (0,)), ((), ()))
NT = (((1,), (1,)), ((), ()))
LOG2E = 1.4426950408889634
HIGHEST = lax.Precision.HIGHEST

NX, NZ, NY, NCORE = 4, 8, 4, 2
GROUP = NX * NZ
PEERS = NY * NCORE
DIMS = 64
PROBES = 64
BLK = 64
CHUNKS = 4
CA = 512
A = CHUNKS * CA
B = 8192
TB = 4096
OWN = 1024


def split3(v):
    h = v.astype(BF16).astype(F32)
    m = (v - h).astype(BF16).astype(F32)
    return h, m, v - h - m


def main_kernel(
    slab_ref, col_ref, probe_ref,
    zsum_ref, lower_ref, trace_ref, sown_ref,
    cols, probes, yt, xall, xaug, kmat, spart, rsrecv, sfull, st,
    zsend, zmine, zcrecv, zyrecv, gsend, grecv,
    in_sem, sz_s, sz_r, sx_s, sx_r, rs_s, rs_r, ag_s, ag_r,
    zc_s, zc_r, zy_s, zy_r, g_s, g_r,
    *, slab_total,
):
    row = lax.axis_index("row")
    col = lax.axis_index("col")
    core = row % 2
    y = (row // 2) % 4
    zhi = row // 8
    z = zhi * 4 + col % 4
    x = col // 4
    mine = y * NCORE + core

    def at_z(r):
        gz = (z + r) % NZ
        return ((gz // 4) * 8 + mine, x * 4 + gz % 4)

    def at_x(r):
        return (row, ((x + r) % NX) * 4 + col % 4)

    me = z * NX + x

    def at_group(g):
        gz = g // NX
        return ((gz // 4) * 8 + mine, (g % NX) * 4 + gz % 4)

    def at_peer(q):
        return (zhi * 8 + q, col)

    def each(lo, hi, f):
        def step(r, _):
            f(r)
            return 0

        lax.fori_loop(lo, hi, step, 0)

    def remote(src, dst, send, recv, device):
        return pltpu.make_async_remote_copy(
            src_ref=src, dst_ref=dst, send_sem=send, recv_sem=recv, device_id=device, device_id_type=MESH
        )

    cp_c = pltpu.make_async_copy(col_ref.at[:, pl.ds(pl.multiple_of(zhi * B, B), B)], cols, in_sem.at[0])
    cp_p = pltpu.make_async_copy(
        probe_ref.at[:, pl.ds(pl.multiple_of(zhi * B, B), B)], probes.at[pl.ds(0, PROBES), :], in_sem.at[1]
    )
    cp_c.start()
    cp_p.start()

    barrier = pltpu.get_barrier_semaphore()

    def greet(device):
        pl.semaphore_signal(barrier, inc=1, device_id=device, device_id_type=MESH)

    each(1, GROUP, lambda r: greet(at_group((me + r) % GROUP)))
    each(1, PEERS, lambda r: greet(at_peer((mine + r) % PEERS)))

    s_in = slab_ref[...].astype(F32)
    xall[x, z] = jnp.concatenate([s_in[: DIMS // 2], s_in[DIMS // 2 :]], axis=1).astype(BF16)
    probes[PROBES:, :] = jnp.zeros((128 - PROBES, B), BF16)

    pl.semaphore_wait(barrier, GROUP - 1 + PEERS - 1)

    def slab_z(r):
        return remote(xall.at[x, z], xall.at[x, z], sz_s.at[r - 1], sz_r.at[r - 1], at_z(r))

    def slab_x(r):
        return remote(xall.at[x], xall.at[x], sx_s.at[r - 1], sx_r.at[r - 1], at_x(r))

    each(1, NZ, lambda r: slab_z(r).start())

    cp_c.wait()
    alpha = LOG2E * 8.0 / DIMS

    def make_yt(i):
        b0 = pl.multiple_of(i * 512, 512)
        yv = cols[:, pl.ds(b0, 512)].astype(F32)
        yp = yv * (2.0 * alpha)
        h, m, l = split3(yp)
        nh, nm, nl = split3(-alpha * jnp.sum(yv * yv, axis=0, keepdims=True))
        r = lax.broadcasted_iota(jnp.int32, (DIMS, 512), 0)
        extra = jnp.where(
            r < 3, 1.0, jnp.where(r == 3, nh, jnp.where(r == 4, nm, jnp.where(r == 5, nl, 0.0)))
        )
        yt[pl.ds(b0, 512), 0:128] = jnp.transpose(jnp.concatenate([h, m], axis=0)).astype(BF16)
        yt[pl.ds(b0, 512), 128:256] = jnp.transpose(jnp.concatenate([l, extra], axis=0)).astype(BF16)

    each(0, B // 1024, make_yt)
    each(1, NZ, lambda r: slab_z(r).wait_recv())
    each(1, NX, lambda r: slab_x(r).start())
    each(B // 1024, B // 512, make_yt)
    cp_p.wait()
    lane = lax.broadcasted_iota(jnp.int32, (DIMS // 2, 128), 1)

    def build_x(c):
        for pair in range(NZ // 2):
            va = xall[c, 2 * pair].astype(F32)
            vb = xall[c, 2 * pair + 1].astype(F32)
            even = jnp.where(lane < 64, va, pltpu.roll(vb, 64, 1))
            odd = jnp.where(lane < 64, pltpu.roll(va, 64, 1), vb)
            xv = jnp.concatenate([even, odd], axis=0)
            nh, nm, nl = split3(-alpha * jnp.sum(xv * xv, axis=0, keepdims=True))
            r = lax.broadcasted_iota(jnp.int32, (DIMS, 128), 0)
            extra = jnp.where(
                r == 0, nh,
                jnp.where(r == 1, nm, jnp.where(r == 2, nl, jnp.where(r < 6, 1.0, 0.0))),
            )
            whole = jnp.concatenate([xv, xv, xv, extra], axis=0).astype(BF16)
            xaug[:, pair * 128 : (pair + 1) * 128] = whole

    def piece(g):
        return (
            pl.ds(pl.multiple_of((g // 4) * 8, 8), 8),
            pl.ds(pl.multiple_of((g % 4) * 128, 128), 128),
        )

    def rs(c, r):
        g = (me + r) % GROUP
        return remote(
            spart.at[(c, *piece(g))], rsrecv.at[c, r - 1], rs_s.at[c], rs_r.at[c], at_group(g)
        )

    def ag(c, r):
        here = sfull.at[(c, *piece(me))]
        return remote(here, here, ag_s.at[c], ag_r.at[c], at_group((me + r) % GROUP))

    def rs_all(c):
        return remote(rsrecv.at[c], rsrecv.at[c], rs_s.at[c], rs_r.at[c], at_z(1))

    def ag_all(c):
        return remote(rsrecv.at[c], rsrecv.at[c], ag_s.at[c], ag_r.at[c], at_z(1))

    def reduce_own(c):
        rs_all(c).wait_recv()
        sfull[(c, *piece(me))] = spart[(c, *piece(me))] + jnp.sum(rsrecv[c], axis=0)
        each(1, GROUP, lambda r: ag(c, r).start())

    def chunk_at(c):
        return pl.ds(pl.multiple_of(c * CA, CA), CA)

    def tile(c, i):
        b0 = pl.multiple_of(i * TB, TB)
        t = lax.dot_general(yt[pl.ds(b0, TB), :], xaug[...], NN, preferred_element_type=F32)
        k = jnp.exp2(t).astype(BF16)
        kmat[pl.ds(b0, TB), chunk_at(c)] = k
        return lax.dot_general(probes[:, pl.ds(b0, TB)], k, NN, preferred_element_type=F32)[:PROBES]

    def clear_part(c):
        spart[c] = jnp.zeros((PROBES, CA), F32)

    each(0, CHUNKS, clear_part)

    def phase1(n):
        index = jnp.where(n == 0, 2 * x, jnp.where(n <= 2 * x, n - 1, n))
        c = index // 2
        half = index % 2

        @pl.when((half == 0) & (c != x))
        def _():
            slab_x((x - c + NX) % NX).wait_recv()

        build_x(c)
        spart[c] += tile(c, half)
        pl.when(half == 1)(lambda: each(1, GROUP, lambda r: rs(c, r).start()))
        pl.when(n == 6)(lambda: reduce_own(0))

    each(0, 2 * CHUNKS, phase1)
    reduce_own(1)
    reduce_own(2)

    wide = lax.broadcasted_iota(jnp.int32, (OWN // 2, 128), 1)
    gsend[...] = jnp.zeros((PROBES, 128), F32)

    def take_chunk(c):
        ag_all(c).wait_recv()
        s = sfull[c]
        hi = s.astype(BF16).astype(F32)
        st[...] = jnp.transpose(jnp.concatenate([hi, s - hi], axis=0)).astype(BF16)
        gsend[:, 0:PROBES] += lax.dot_general(s, s, NT, precision=HIGHEST, preferred_element_type=F32)

    def image_part(c, o):
        zt = lax.dot_general(
            kmat[pl.ds(pl.multiple_of(o * OWN, OWN), OWN), chunk_at(c)], st[...], NN,
            preferred_element_type=F32,
        )
        u = zt + pltpu.roll(zt, 64, 1)
        return jnp.where(wide < 64, u[: OWN // 2], u[OWN // 2 :])

    def both(c, t):
        yo = (y + 1 + t) % NY
        zsend[t] += image_part(c, yo * 2 + 1 - core)
        zmine[t] += image_part(c, yo * 2 + core)

    def clear(t):
        zsend[t] = jnp.zeros((OWN // 2, 128), F32)
        zmine[t] = jnp.zeros((OWN // 2, 128), F32)

    each(0, NY, clear)

    def one_pass(c):
        take_chunk(c)
        each(0, 2, lambda t: both(c, t))
        pl.when(c == 0)(lambda: reduce_own(3))
        each(2, NY, lambda t: both(c, t))

    each(0, CHUNKS - 1, one_pass)
    take_chunk(CHUNKS - 1)

    def g_copy(r):
        return remote(
            gsend, grecv.at[r - 1], g_s.at[r - 1], g_r.at[r - 1], at_peer((mine + r) % PEERS)
        )

    each(1, PEERS, lambda r: g_copy(r).start())

    def zc(t):
        return remote(zsend.at[t], zcrecv.at[t], zc_s.at[t], zc_r.at[t], at_peer(y * 2 + 1 - core))

    def zy(t):
        return remote(
            zmine.at[t], zyrecv.at[t], zy_s.at[t], zy_r.at[t], at_peer(((y + 1 + t) % NY) * 2 + core)
        )

    def last_pass(t):
        yo = (y + 1 + t) % NY
        zsend[t] += image_part(CHUNKS - 1, yo * 2 + 1 - core)
        zc(t).start()
        own = image_part(CHUNKS - 1, yo * 2 + core)
        zc(t).wait_recv()
        zmine[t] += own + zcrecv[t]
        pl.when(t < NY - 1)(lambda: zy(t).start())

    each(0, NY, last_pass)

    each(1, PEERS, lambda r: g_copy(r).wait_send())
    each(1, PEERS, lambda r: g_copy(r).wait_recv())
    total = gsend[...]
    for r in range(PEERS - 1):
        total = total + grecv[r]
    gram = total / slab_total
    glane = lax.broadcasted_iota(jnp.int32, (PROBES, 128), 1)
    grow = lax.broadcasted_iota(jnp.int32, (PROBES, 128), 0)
    trace_ref[...] = jnp.full((8, 128), jnp.sum(jnp.where(glane == grow, gram, 0.0)))
    m = jnp.where(glane < 64, gram, jnp.where(glane - 64 == grow, 1.0, 0.0))
    for k in range(PROBES - 1):
        pivot = m[k : k + 1, :]
        factor = m[:, k : k + 1] / m[k : k + 1, k : k + 1]
        m = m - jnp.where(grow > k, factor * pivot, 0.0)
    d = jnp.sum(jnp.where(glane == grow, m, 0.0), axis=1, keepdims=True)
    lower_ref[...] = jnp.where(glane >= 64, m / jnp.sqrt(d), 0.0)

    own_lanes = pl.ds(pl.multiple_of((z // 2) * 128, 128), 128)
    stile = sfull[x, :, own_lanes]
    sown_ref[...] = jnp.where(z % 2 == 1, pltpu.roll(stile, 64, 1), stile)

    each(1, NZ, lambda r: slab_z(r).wait_send())
    each(1, NX, lambda r: slab_x(r).wait_send())

    each(0, CHUNKS, lambda c: rs_all(c).wait_send())
    each(0, CHUNKS, lambda c: ag_all(c).wait_send())
    each(0, NY, lambda t: zc(t).wait_send())
    each(0, NY - 1, lambda t: zy(t).wait())
    zsum_ref[...] = zmine[NY - 1] + (zyrecv[0] + zyrecv[1] + zyrecv[2])


def final_kernel(zsum_ref, upper_ref, trace_ref, sown_ref, basis_ref, image_ref, *, slab_total, point_total):
    upper = upper_ref[...]
    lower = pltpu.roll(upper, 64, 1)
    basis = lax.dot_general(
        lower[:, :64], sown_ref[...], NN, precision=HIGHEST, preferred_element_type=F32
    )
    basis_ref[...] = basis[:, :64].astype(BF16)
    scale = jnp.sqrt(jnp.float32(PROBES * point_total) / trace_ref[0:1, 0:1]) / slab_total
    zs = zsum_ref[...]
    for half, w in ((0, lower), (1, upper)):
        image_ref[:, half * 512 : half * 512 + 512] = scale * lax.dot_general(
            w, zs, NT, precision=HIGHEST, preferred_element_type=F32
        )


def body(slab_points, col_points, probes):
    vmem = pl.BlockSpec(memory_space=pltpu.VMEM)
    hbm = pl.BlockSpec(memory_space=pl.ANY)
    dma = pltpu.SemaphoreType.DMA
    zsum, lower, trace, sown = pl.pallas_call(
        functools.partial(main_kernel, slab_total=A * PEERS),
        out_shape=(
            jax.ShapeDtypeStruct((OWN // 2, 128), F32),
            jax.ShapeDtypeStruct((PROBES, 128), F32),
            jax.ShapeDtypeStruct((8, 128), F32),
            jax.ShapeDtypeStruct((PROBES, 128), F32),
        ),
        in_specs=[vmem, hbm, hbm],
        out_specs=(vmem, vmem, vmem, vmem),
        scratch_shapes=[
            pltpu.VMEM((DIMS, B), BF16),
            pltpu.VMEM((128, B), BF16),
            pltpu.VMEM((B, 256), BF16),
            pltpu.VMEM((NX, NZ, 32, 128), BF16),
            pltpu.VMEM((256, CA), BF16),
            pltpu.VMEM((B, A), BF16),
            pltpu.VMEM((CHUNKS, PROBES, CA), F32),
            pltpu.VMEM((CHUNKS, GROUP - 1, 8, 128), F32),
            pltpu.VMEM((CHUNKS, PROBES, CA), F32),
            pltpu.VMEM((CA, 128), BF16),
            pltpu.VMEM((NY, OWN // 2, 128), F32),
            pltpu.VMEM((NY, OWN // 2, 128), F32),
            pltpu.VMEM((NY, OWN // 2, 128), F32),
            pltpu.VMEM((NY - 1, OWN // 2, 128), F32),
            pltpu.VMEM((PROBES, 128), F32),
            pltpu.VMEM((PEERS - 1, PROBES, 128), F32),
            dma((2,)),
            dma((NZ - 1,)), dma((NZ - 1,)), dma((NX - 1,)), dma((NX - 1,)),
            dma((CHUNKS,)), dma((CHUNKS,)), dma((CHUNKS,)), dma((CHUNKS,)),
            dma((NY,)), dma((NY,)), dma((NY - 1,)), dma((NY - 1,)),
            dma((PEERS - 1,)), dma((PEERS - 1,)),
        ],
        compiler_params=pltpu.CompilerParams(
            collective_id=0, has_side_effects=True, vmem_limit_bytes=62 << 20
        ),
        name="slab_kernel",
    )(slab_points, col_points, probes)
    return pl.pallas_call(
        functools.partial(final_kernel, slab_total=A * PEERS, point_total=B * GROUP),
        out_shape=(
            jax.ShapeDtypeStruct((PROBES, BLK), BF16),
            jax.ShapeDtypeStruct((PROBES, OWN), F32),
        ),
        in_specs=[vmem, vmem, vmem, vmem],
        out_specs=(vmem, vmem),
        name="image_kernel",
    )(zsum, lower, trace, sown)


def solution(mesh):
    return jax.shard_map(
        body,
        mesh=mesh,
        in_specs=(P(None, ("row", "col")), P(None, "col"), P(None, "col")),
        out_specs=(P(None, ("row", "col")), P(None, ("col", "row"))),
        check_vma=False,
    )
```

time: 505 us -> 79 us (0.16)
  waiting for transfers between devices: 268 us -> 0 us
  blocking collectives: 117 us -> 0 us
  Pallas kernels: 0 us -> 78.2 us
  matrix products: 70.4 us -> 0 us
  other arithmetic: 16.7 us -> 0 us
  between operations: 14.9 us -> 0.64 us
  local copies, waits for them, and re-layouts: 9.43 us -> 0 us
  loops' own time: 5.54 us -> 0 us
    psum x1 -> x0, waiting for transfers between devices: 155 us -> none  [body(): sample = lax.psum(partial_value, 'col')]
    reduce_scatter x1 -> x0, waiting for transfers between devices: 113 us -> none  [body(): lax.psum_scatter(terms, 'row', scatter_dimension=1, tiled=True)]
    psum x1 -> x0, blocking collectives: 78.8 us -> none  [body(): lax.psum(jnp.dot(sample, sample.T, precision=lax.Precision.HIGHEST), 'row')]
    pallas_call x0 -> x2, Pallas kernels: none -> 78.2 us  [the longest x1 75.8 us: body(): pl.pallas_call(functools.partial(main_kernel, slab_total=A * PEERS), out_...]
    dot_general x17 -> x0, matrix products: 69 us -> none  [the longest x8 35.2 us: image_step(): block_out = jnp.dot(basis_full, kernel, preferred_element_type=jnp.float32)]
    all_gather x1 -> x0, blocking collectives: 38.4 us -> none  [body(): slab_whole = lax.all_gather(slab_points, 'col', axis=1, tiled=True)]
    another operation x5 -> x0, other arithmetic: 12.1 us -> none  [the longest x3 6.58 us: body(): lower = jnp.linalg.cholesky(gram)]
    another operation x2 -> x0, loops' own time: 5.54 us -> none  [the longest x1 5.54 us: body(): lax.scan(sample_step, empty, jnp.arange(blocks, dtype=jnp.int32))]
  transfers between devices with their start and end apart: 2 -> 0, of which waited for: 2 -> 0; matrix products, arithmetic and copies ran while one was open for 0% -> 0% of each run, Pallas kernels for 0% -> 0%
where the time goes in v2:
time: 79 us; the launch traced here: 78.8 us
  Pallas kernels  78.2 us (99%)
    pallas_call x1, Pallas kernels, body(): pl.pallas_call(functools.partial(main_kernel, slab_total=A * PEERS), out_...  75.8 us
    pallas_call x1, Pallas kernels, body(): pl.pallas_call(functools.partial(final_kernel, slab_total=A * PEERS, poin...  2.33 us

profile of v2, /device:TPU:9, one launch (start us, length us, event | category | flops | bytes accessed | tf_op | source)
XLA Modules:
  0.0 78.8 jit_solution(3210730160171301194)
XLA Ops:
  0.6 75.8 %slab_kernel.1 = (f32[512,128]{1,0:T(8,128)}, f32[64,128]{1,0:T(8,128)}, f32[8,128]{1,0:T(8,128)}, f32[64,128]{1,0:T(8,128)}) custom-call(bf16[64,64]{1,0:T(8,128)(2,1)} %slab_ref.1, bf16[64,16384]{1,0:T(8,128)(2,1)} %col_ref.1, bf16[64,16384]{1,0:T(8,128)(2,1)} %probe_ref.1), custom_call_target="tpu_custom_call" | custom-call | tf_op jit(solution)/shard_map/slab_kernel/pallas_call | solution.py:327
  76.5 2.3 %image_kernel.1 = (bf16[64,64]{1,0:T(8,128)(2,1)}, f32[64,1024]{1,0:T(8,128)}) custom-call(f32[512,128]{1,0:T(8,128)} %get-tuple-element.6.zsum_ref, f32[64,128]{1,0:T(8,128)} %get-tuple-element.7.upper_ref, f32[8,128]{1,0:T(8,128)} %get-tuple-element.8.trace_ref, f32[64,128]{1,0:T(8,128)} %get-tuple-element.9.sown_ref), custom_call_target="tpu_custom_call" | custom-call | tf_op jit(solution)/shard_map/image_kernel/pallas_call | solution.py:365

commit v3 on v2

--- a/solution.py
+++ b/solution.py
@@ -38,12 +38,12 @@
 
 def main_kernel(
     slab_ref, col_ref, probe_ref,
-    zsum_ref, lower_ref, trace_ref, sown_ref,
+    basis_ref, image_ref,
     cols, probes, yt, xall, xaug, kmat, spart, rsrecv, sfull, st,
-    zsend, zmine, zcrecv, zyrecv, gsend, grecv,
+    zacc, zsend, zmine, zcrecv, zout, zyrecv, gacc, gall, tmat, tinv,
     in_sem, sz_s, sz_r, sx_s, sx_r, rs_s, rs_r, ag_s, ag_r,
     zc_s, zc_r, zy_s, zy_r, g_s, g_r,
-    *, slab_total,
+    *, slab_total, point_total,
 ):
     row = lax.axis_index("row")
     col = lax.axis_index("col")
@@ -132,6 +132,7 @@
     each(1, NX, lambda r: slab_x(r).start())
     each(B // 1024, B // 512, make_yt)
     cp_p.wait()
+
     lane = lax.broadcasted_iota(jnp.int32, (DIMS // 2, 128), 1)
 
     def build_x(c):
@@ -207,93 +208,161 @@
         pl.when(n == 6)(lambda: reduce_own(0))
 
     each(0, 2 * CHUNKS, phase1)
-    reduce_own(1)
-    reduce_own(2)
+    each(1, CHUNKS, reduce_own)
 
     wide = lax.broadcasted_iota(jnp.int32, (OWN // 2, 128), 1)
-    gsend[...] = jnp.zeros((PROBES, 128), F32)
+    glane = lax.broadcasted_iota(jnp.int32, (PROBES, 128), 1)
+    grow = lax.broadcasted_iota(jnp.int32, (PROBES, 128), 0)
+    gacc[...] = jnp.zeros((PROBES, 128), F32)
 
     def take_chunk(c):
         ag_all(c).wait_recv()
         s = sfull[c]
         hi = s.astype(BF16).astype(F32)
         st[...] = jnp.transpose(jnp.concatenate([hi, s - hi], axis=0)).astype(BF16)
-        gsend[:, 0:PROBES] += lax.dot_general(s, s, NT, precision=HIGHEST, preferred_element_type=F32)
-
-    def image_part(c, o):
-        zt = lax.dot_general(
-            kmat[pl.ds(pl.multiple_of(o * OWN, OWN), OWN), chunk_at(c)], st[...], NN,
+
+    def add_gram(c):
+        s = sfull[c]
+        gacc[:, 0:PROBES] += lax.dot_general(s, s, NT, precision=HIGHEST, preferred_element_type=F32)
+
+    def g_copy(p, r):
+        return remote(
+            gall.at[p, mine], gall.at[p, mine], g_s.at[p * PEERS + r], g_r.at[p * PEERS + r],
+            at_peer((mine + r) % PEERS),
+        )
+
+    def send_gram(p):
+        v = gacc[...]
+        gall[p, mine] = jnp.where(
+            glane[:32] < 64, v[:32], pltpu.roll(v[32:], 64, 1)
+        )
+        each(1, PEERS, lambda r: g_copy(p, r).start())
+
+    def sum_gram(p):
+        each(1, PEERS, lambda r: g_copy(p, r).wait_recv())
+        v = jnp.sum(gall[p], axis=0)
+        both_halves = jnp.concatenate([v, pltpu.roll(v, 64, 1)], axis=0)
+        return jnp.where(glane < 64, both_halves, 0.0)
+
+    def damping():
+        m = sum_gram(0)
+
+        def trace(v):
+            return jnp.sum(jnp.where(glane == grow, v, 0.0), keepdims=True)
+
+        m = m / jnp.maximum(trace(m), 1e-30)
+        for _ in range(3):
+            m = lax.dot_general(m[:, :PROBES], m, NN, precision=HIGHEST, preferred_element_type=F32)
+            m = m / jnp.maximum(trace(m), 1e-30)
+        diag = jnp.where(glane == grow, m, 0.0)
+        top = jnp.max(diag, keepdims=True)
+        ucol = jnp.sum(
+            jnp.where(jnp.sum(diag, axis=0, keepdims=True) == top, jnp.where(glane < 64, m, 0.0), 0.0),
+            axis=1, keepdims=True,
+        )
+        urow = jnp.sum(
+            jnp.where(jnp.sum(diag, axis=1, keepdims=True) == top, m, 0.0), axis=0, keepdims=True
+        )
+        uu = jnp.maximum(jnp.sum(ucol * ucol, axis=0, keepdims=True), 1e-30)
+        outer = ucol * (urow + pltpu.roll(urow, 64, 1)) / uu
+        eye = jnp.where((glane == grow) | (glane - 64 == grow), 1.0, 0.0)
+        t = eye - 0.875 * outer
+        tinv[...] = eye + 7.0 * outer
+        tmat[0:PROBES, :] = jnp.where(glane < 64, t, 0.0)
+        tmat[PROBES:128, :] = jnp.where(glane >= 64, t, 0.0)
+
+    def image_part(c, t):
+        yo = (y + 1 + t) % NY
+        return lax.dot_general(
+            kmat[pl.ds(pl.multiple_of(yo * 2 * OWN, 2 * OWN), 2 * OWN), chunk_at(c)], st[...], NN,
             preferred_element_type=F32,
         )
-        u = zt + pltpu.roll(zt, 64, 1)
-        return jnp.where(wide < 64, u[: OWN // 2], u[OWN // 2 :])
-
-    def both(c, t):
-        yo = (y + 1 + t) % NY
-        zsend[t] += image_part(c, yo * 2 + 1 - core)
-        zmine[t] += image_part(c, yo * 2 + core)
-
-    def clear(t):
-        zsend[t] = jnp.zeros((OWN // 2, 128), F32)
-        zmine[t] = jnp.zeros((OWN // 2, 128), F32)
-
-    each(0, NY, clear)
+
+    def merged(t, o):
+        u = zacc[t, pl.ds(pl.multiple_of(o * OWN, OWN), OWN // 2), :]
+        v = zacc[t, pl.ds(pl.multiple_of(o * OWN + OWN // 2, OWN // 2), OWN // 2), :]
+        return jnp.where(wide < 64, u + pltpu.roll(u, 64, 1), v + pltpu.roll(v, 64, 1))
+
+    def add_part(c, t):
+        zacc[t] += image_part(c, t)
+
+    def first_part(t):
+        zacc[t] = image_part(0, t)
 
     def one_pass(c):
         take_chunk(c)
-        each(0, 2, lambda t: both(c, t))
-        pl.when(c == 0)(lambda: reduce_own(3))
-        each(2, NY, lambda t: both(c, t))
-
-    each(0, CHUNKS - 1, one_pass)
+        add_gram(c)
+        each(0, NY, lambda t: add_part(c, t))
+
+    take_chunk(0)
+    add_gram(0)
+    send_gram(0)
+    each(0, NY, first_part)
+    each(1, CHUNKS - 1, one_pass)
+    damping()
     take_chunk(CHUNKS - 1)
-
-    def g_copy(r):
-        return remote(
-            gsend, grecv.at[r - 1], g_s.at[r - 1], g_r.at[r - 1], at_peer((mine + r) % PEERS)
-        )
-
-    each(1, PEERS, lambda r: g_copy(r).start())
+    add_gram(CHUNKS - 1)
+    send_gram(1)
 
     def zc(t):
         return remote(zsend.at[t], zcrecv.at[t], zc_s.at[t], zc_r.at[t], at_peer(y * 2 + 1 - core))
 
     def zy(t):
         return remote(
-            zmine.at[t], zyrecv.at[t], zy_s.at[t], zy_r.at[t], at_peer(((y + 1 + t) % NY) * 2 + core)
-        )
-
-    def last_pass(t):
-        yo = (y + 1 + t) % NY
-        zsend[t] += image_part(CHUNKS - 1, yo * 2 + 1 - core)
+            zout.at[t], zyrecv.at[t], zy_s.at[t], zy_r.at[t], at_peer(((y + 1 + t) % NY) * 2 + core)
+        )
+
+    def last_part(t):
+        add_part(CHUNKS - 1, t)
+        zsend[t] = merged(t, 1 - core)
         zc(t).start()
-        own = image_part(CHUNKS - 1, yo * 2 + core)
+
+    def damped(t):
         zc(t).wait_recv()
-        zmine[t] += own + zcrecv[t]
-        pl.when(t < NY - 1)(lambda: zy(t).start())
-
-    each(0, NY, last_pass)
-
-    each(1, PEERS, lambda r: g_copy(r).wait_send())
-    each(1, PEERS, lambda r: g_copy(r).wait_recv())
-    total = gsend[...]
-    for r in range(PEERS - 1):
-        total = total + grecv[r]
-    gram = total / slab_total
-    glane = lax.broadcasted_iota(jnp.int32, (PROBES, 128), 1)
-    grow = lax.broadcasted_iota(jnp.int32, (PROBES, 128), 0)
-    trace_ref[...] = jnp.full((8, 128), jnp.sum(jnp.where(glane == grow, gram, 0.0)))
-    m = jnp.where(glane < 64, gram, jnp.where(glane - 64 == grow, 1.0, 0.0))
-    for k in range(PROBES - 1):
-        pivot = m[k : k + 1, :]
-        factor = m[:, k : k + 1] / m[k : k + 1, k : k + 1]
-        m = m - jnp.where(grow > k, factor * pivot, 0.0)
+        return lax.dot_general(
+            merged(t, core) + zcrecv[t], tmat[...], NN, precision=HIGHEST, preferred_element_type=F32
+        )
+
+    def share(t):
+        zout[t] = damped(t).astype(BF16)
+        zy(t).start()
+
+    each(0, NY, last_part)
+    each(0, NY - 1, share)
+    zmine[...] = damped(NY - 1)
+
+    gram = sum_gram(1) / slab_total
+    trace = jnp.sum(jnp.where(glane == grow, gram, 0.0), keepdims=True)
+    m = jnp.where(glane < 64, gram, tinv[...])
+    for k in range(0, PROBES, 8):
+        cs, fs, rows = [], [], []
+        for i in range(8):
+            q = k + i
+            c = jnp.broadcast_to(m[:, q : q + 1], (PROBES, 128))
+            r = m[q : q + 1, :]
+            for j in range(i):
+                c = c - fs[j] * cs[j][q : q + 1, :]
+                r = r - fs[j][q : q + 1, :] * rows[j]
+            cs.append(c)
+            fs.append(jnp.where(grow > q, c / c[q : q + 1, :], 0.0))
+            rows.append(r)
+        for f, r in zip(fs, rows):
+            m = m - f * r
     d = jnp.sum(jnp.where(glane == grow, m, 0.0), axis=1, keepdims=True)
-    lower_ref[...] = jnp.where(glane >= 64, m / jnp.sqrt(d), 0.0)
+    upper = jnp.where(glane >= 64, m / jnp.sqrt(d), 0.0)
+    lower = pltpu.roll(upper, 64, 1)
 
     own_lanes = pl.ds(pl.multiple_of((z // 2) * 128, 128), 128)
     stile = sfull[x, :, own_lanes]
-    sown_ref[...] = jnp.where(z % 2 == 1, pltpu.roll(stile, 64, 1), stile)
+    sown = jnp.where(z % 2 == 1, pltpu.roll(stile, 64, 1), stile)
+    sdamp = lax.dot_general(
+        tmat[0:PROBES, 0:PROBES], sown, NN, precision=HIGHEST, preferred_element_type=F32
+    )
+    basis = lax.dot_general(
+        lower[:, :PROBES], sdamp, NN, precision=HIGHEST, preferred_element_type=F32
+    )
+    basis_ref[...] = basis[:, :BLK].astype(BF16)
+    scale = jnp.sqrt(jnp.float32(PROBES * point_total) / trace) / slab_total
 
     each(1, NZ, lambda r: slab_z(r).wait_send())
     each(1, NX, lambda r: slab_x(r).wait_send())
@@ -301,39 +370,32 @@
     each(0, CHUNKS, lambda c: rs_all(c).wait_send())
     each(0, CHUNKS, lambda c: ag_all(c).wait_send())
     each(0, NY, lambda t: zc(t).wait_send())
+    each(0, 2, lambda p: each(1, PEERS, lambda r: g_copy(p, r).wait_send()))
     each(0, NY - 1, lambda t: zy(t).wait())
-    zsum_ref[...] = zmine[NY - 1] + (zyrecv[0] + zyrecv[1] + zyrecv[2])
-
-
-def final_kernel(zsum_ref, upper_ref, trace_ref, sown_ref, basis_ref, image_ref, *, slab_total, point_total):
-    upper = upper_ref[...]
-    lower = pltpu.roll(upper, 64, 1)
-    basis = lax.dot_general(
-        lower[:, :64], sown_ref[...], NN, precision=HIGHEST, preferred_element_type=F32
-    )
-    basis_ref[...] = basis[:, :64].astype(BF16)
-    scale = jnp.sqrt(jnp.float32(PROBES * point_total) / trace_ref[0:1, 0:1]) / slab_total
-    zs = zsum_ref[...]
+    zs = zmine[...] + (zyrecv[0].astype(F32) + zyrecv[1].astype(F32) + zyrecv[2].astype(F32))
     for half, w in ((0, lower), (1, upper)):
         image_ref[:, half * 512 : half * 512 + 512] = scale * lax.dot_general(
             w, zs, NT, precision=HIGHEST, preferred_element_type=F32
         )
+
+
+def finish_kernel(basis_in, image_in, basis_out, image_out):
+    basis_out[...] = basis_in[...]
+    image_out[...] = image_in[...]
 
 
 def body(slab_points, col_points, probes):
     vmem = pl.BlockSpec(memory_space=pltpu.VMEM)
     hbm = pl.BlockSpec(memory_space=pl.ANY)
     dma = pltpu.SemaphoreType.DMA
-    zsum, lower, trace, sown = pl.pallas_call(
-        functools.partial(main_kernel, slab_total=A * PEERS),
+    basis, image = pl.pallas_call(
+        functools.partial(main_kernel, slab_total=A * PEERS, point_total=B * GROUP),
         out_shape=(
-            jax.ShapeDtypeStruct((OWN // 2, 128), F32),
-            jax.ShapeDtypeStruct((PROBES, 128), F32),
-            jax.ShapeDtypeStruct((8, 128), F32),
-            jax.ShapeDtypeStruct((PROBES, 128), F32),
+            jax.ShapeDtypeStruct((PROBES, BLK), BF16),
+            jax.ShapeDtypeStruct((PROBES, OWN), F32),
         ),
         in_specs=[vmem, hbm, hbm],
-        out_specs=(vmem, vmem, vmem, vmem),
+        out_specs=(vmem, vmem),
         scratch_shapes=[
             pltpu.VMEM((DIMS, B), BF16),
             pltpu.VMEM((128, B), BF16),
@@ -345,17 +407,21 @@
             pltpu.VMEM((CHUNKS, GROUP - 1, 8, 128), F32),
             pltpu.VMEM((CHUNKS, PROBES, CA), F32),
             pltpu.VMEM((CA, 128), BF16),
+            pltpu.VMEM((NY, 2 * OWN, 128), F32),
             pltpu.VMEM((NY, OWN // 2, 128), F32),
+            pltpu.VMEM((OWN // 2, 128), F32),
             pltpu.VMEM((NY, OWN // 2, 128), F32),
-            pltpu.VMEM((NY, OWN // 2, 128), F32),
-            pltpu.VMEM((NY - 1, OWN // 2, 128), F32),
+            pltpu.VMEM((NY - 1, OWN // 2, 128), BF16),
+            pltpu.VMEM((NY - 1, OWN // 2, 128), BF16),
             pltpu.VMEM((PROBES, 128), F32),
-            pltpu.VMEM((PEERS - 1, PROBES, 128), F32),
+            pltpu.VMEM((2, PEERS, 32, 128), F32),
+            pltpu.VMEM((128, 128), F32),
+            pltpu.VMEM((PROBES, 128), F32),
             dma((2,)),
             dma((NZ - 1,)), dma((NZ - 1,)), dma((NX - 1,)), dma((NX - 1,)),
             dma((CHUNKS,)), dma((CHUNKS,)), dma((CHUNKS,)), dma((CHUNKS,)),
             dma((NY,)), dma((NY,)), dma((NY - 1,)), dma((NY - 1,)),
-            dma((PEERS - 1,)), dma((PEERS - 1,)),
+            dma((2 * PEERS,)), dma((2 * PEERS,)),
         ],
         compiler_params=pltpu.CompilerParams(
             collective_id=0, has_side_effects=True, vmem_limit_bytes=62 << 20
@@ -363,15 +429,15 @@
         name="slab_kernel",
     )(slab_points, col_points, probes)
     return pl.pallas_call(
-        functools.partial(final_kernel, slab_total=A * PEERS, point_total=B * GROUP),
+        finish_kernel,
         out_shape=(
             jax.ShapeDtypeStruct((PROBES, BLK), BF16),
             jax.ShapeDtypeStruct((PROBES, OWN), F32),
         ),
-        in_specs=[vmem, vmem, vmem, vmem],
+        in_specs=[vmem, vmem],
         out_specs=(vmem, vmem),
-        name="image_kernel",
-    )(zsum, lower, trace, sown)
+        name="finish",
+    )(basis, image)
 
 
 def solution(mesh):

time: 79 us -> 75.7 us (0.958)
  Pallas kernels: 78.2 us -> 74.8 us
    pallas_call x2, Pallas kernels: 78.2 us -> 74.8 us  [the longest x1 73.1 us: body(): pl.pallas_call(functools.partial(main_kernel, slab_total=A * PEERS, point...]
where the time goes in v3:
time: 75.7 us; the launch traced here: 75.4 us
  Pallas kernels  74.8 us (99%)
    pallas_call x1, Pallas kernels, body(): pl.pallas_call(functools.partial(main_kernel, slab_total=A * PEERS, point...  73.1 us
    pallas_call x1, Pallas kernels, body(): pl.pallas_call(finish_kernel, out_shape=(jax.ShapeDtypeStruct((PROBES, BL...  1.69 us

profile of v3, /device:TPU:9, one launch (start us, length us, event | category | flops | bytes accessed | tf_op | source)
XLA Modules:
  0.0 75.4 jit_solution(10523100278632403982)
XLA Ops:
  0.6 73.1 %slab_kernel.1 = (bf16[64,64]{1,0:T(8,128)(2,1)}, f32[64,1024]{1,0:T(8,128)}) custom-call(bf16[64,64]{1,0:T(8,128)(2,1)} %slab_ref.1, bf16[64,16384]{1,0:T(8,128)(2,1)} %col_ref.1, bf16[64,16384]{1,0:T(8,128)(2,1)} %probe_ref.1), custom_call_target="tpu_custom_call" | custom-call | tf_op jit(solution)/shard_map/slab_kernel/pallas_call | solution.py:391
  73.7 1.7 %finish.1 = (bf16[64,64]{1,0:T(8,128)(2,1)}, f32[64,1024]{1,0:T(8,128)}) custom-call(bf16[64,64]{1,0:T(8,128)(2,1)} %get-tuple-element.4.basis_in, f32[64,1024]{1,0:T(8,128)} %get-tuple-element.5.image_in), custom_call_target="tpu_custom_call" | custom-call | tf_op jit(solution)/shard_map/finish/pallas_call | solution.py:431

commit v4 on v3

--- a/solution.py
+++ b/solution.py
@@ -19,6 +19,10 @@
 NX, NZ, NY, NCORE = 4, 8, 4, 2
 GROUP = NX * NZ
 PEERS = NY * NCORE
+OTHERS = sorted(
+    ((dx, dz) for dx in range(NX) for dz in range(NZ) if dx or dz),
+    key=lambda o: (-min(o[0], NX - o[0]) - min(o[1], NZ - o[1]), o),
+)
 DIMS = 64
 PROBES = 64
 BLK = 64
@@ -28,6 +32,21 @@
 B = 8192
 TB = 4096
 OWN = 1024
+
+
+def split2(v):
+    h = v.astype(BF16)
+    return h, (v - h.astype(F32)).astype(BF16)
+
+
+def dot3(a, b, dims):
+    ah, al = split2(a)
+    bh, bl = split2(b)
+
+    def one(u, v):
+        return lax.dot_general(u, v, dims, preferred_element_type=F32)
+
+    return one(ah, bh) + (one(ah, bl) + one(al, bh))
 
 
 def split3(v):
@@ -47,25 +66,22 @@
 ):
     row = lax.axis_index("row")
     col = lax.axis_index("col")
-    core = row % 2
-    y = (row // 2) % 4
-    zhi = row // 8
-    z = zhi * 4 + col % 4
-    x = col // 4
+    core = lax.rem(row, 2)
+    y = lax.rem(lax.div(row, 2), 4)
+    zhi = lax.div(row, 8)
+    z = zhi * 4 + lax.rem(col, 4)
+    x = lax.div(col, 4)
     mine = y * NCORE + core
 
     def at_z(r):
-        gz = (z + r) % NZ
-        return ((gz // 4) * 8 + mine, x * 4 + gz % 4)
+        return at_offset(0, r)
 
     def at_x(r):
-        return (row, ((x + r) % NX) * 4 + col % 4)
-
-    me = z * NX + x
-
-    def at_group(g):
-        gz = g // NX
-        return ((gz // 4) * 8 + mine, (g % NX) * 4 + gz % 4)
+        return at_offset(r, 0)
+
+    def at_offset(dx, dz):
+        gx, gz = lax.rem(x + dx, NX), lax.rem(z + dz, NZ)
+        return (lax.div(gz, 4) * 8 + mine, gx * 4 + lax.rem(gz, 4))
 
     def at_peer(q):
         return (zhi * 8 + q, col)
@@ -76,6 +92,10 @@
             return 0
 
         lax.fori_loop(lo, hi, step, 0)
+
+    def unrolled(lo, hi, f):
+        for r in range(lo, hi):
+            f(r)
 
     def remote(src, dst, send, recv, device):
         return pltpu.make_async_remote_copy(
@@ -94,8 +114,9 @@
     def greet(device):
         pl.semaphore_signal(barrier, inc=1, device_id=device, device_id_type=MESH)
 
-    each(1, GROUP, lambda r: greet(at_group((me + r) % GROUP)))
-    each(1, PEERS, lambda r: greet(at_peer((mine + r) % PEERS)))
+    for dx, dz in OTHERS:
+        greet(at_offset(dx, dz))
+    unrolled(1, PEERS, lambda r: greet(at_peer(lax.rem(mine + r, PEERS))))
 
     s_in = slab_ref[...].astype(F32)
     xall[x, z] = jnp.concatenate([s_in[: DIMS // 2], s_in[DIMS // 2 :]], axis=1).astype(BF16)
@@ -109,7 +130,8 @@
     def slab_x(r):
         return remote(xall.at[x], xall.at[x], sx_s.at[r - 1], sx_r.at[r - 1], at_x(r))
 
-    each(1, NZ, lambda r: slab_z(r).start())
+    for r in (4, 3, 5, 2, 6, 1, 7):
+        slab_z(r).start()
 
     cp_c.wait()
     alpha = LOG2E * 8.0 / DIMS
@@ -128,8 +150,9 @@
         yt[pl.ds(b0, 512), 128:256] = jnp.transpose(jnp.concatenate([l, extra], axis=0)).astype(BF16)
 
     each(0, B // 1024, make_yt)
-    each(1, NZ, lambda r: slab_z(r).wait_recv())
-    each(1, NX, lambda r: slab_x(r).start())
+    unrolled(1, NZ, lambda r: slab_z(r).wait_recv())
+    for r in (2, 1, 3):
+        slab_x(r).start()
     each(B // 1024, B // 512, make_yt)
     cp_p.wait()
 
@@ -151,21 +174,25 @@
             whole = jnp.concatenate([xv, xv, xv, extra], axis=0).astype(BF16)
             xaug[:, pair * 128 : (pair + 1) * 128] = whole
 
-    def piece(g):
+    def piece(gx, gz):
         return (
-            pl.ds(pl.multiple_of((g // 4) * 8, 8), 8),
-            pl.ds(pl.multiple_of((g % 4) * 128, 128), 128),
-        )
-
-    def rs(c, r):
-        g = (me + r) % GROUP
+            pl.ds(pl.multiple_of(gz * 8, 8), 8), pl.ds(pl.multiple_of(gx * 128, 128), 128)
+        )
+
+    def rs(c, k):
+        dx, dz = OTHERS[k]
+        there = piece(lax.rem(x + dx, NX), lax.rem(z + dz, NZ))
         return remote(
-            spart.at[(c, *piece(g))], rsrecv.at[c, r - 1], rs_s.at[c], rs_r.at[c], at_group(g)
-        )
-
-    def ag(c, r):
-        here = sfull.at[(c, *piece(me))]
-        return remote(here, here, ag_s.at[c], ag_r.at[c], at_group((me + r) % GROUP))
+            spart.at[(c, *there)], rsrecv.at[c, k], rs_s.at[c], rs_r.at[c], at_offset(dx, dz)
+        )
+
+    def ag(c, k):
+        here = sfull.at[(c, *piece(x, z))]
+        return remote(here, here, ag_s.at[c], ag_r.at[c], at_offset(*OTHERS[k]))
+
+    def to_others(f):
+        for k in range(GROUP - 1):
+            f(k)
 
     def rs_all(c):
         return remote(rsrecv.at[c], rsrecv.at[c], rs_s.at[c], rs_r.at[c], at_z(1))
@@ -175,8 +202,8 @@
 
     def reduce_own(c):
         rs_all(c).wait_recv()
-        sfull[(c, *piece(me))] = spart[(c, *piece(me))] + jnp.sum(rsrecv[c], axis=0)
-        each(1, GROUP, lambda r: ag(c, r).start())
+        sfull[(c, *piece(x, z))] = spart[(c, *piece(x, z))] + jnp.sum(rsrecv[c], axis=0)
+        to_others(lambda k: ag(c, k).start())
 
     def chunk_at(c):
         return pl.ds(pl.multiple_of(c * CA, CA), CA)
@@ -204,11 +231,12 @@
 
         build_x(c)
         spart[c] += tile(c, half)
-        pl.when(half == 1)(lambda: each(1, GROUP, lambda r: rs(c, r).start()))
+        pl.when(half == 1)(lambda: to_others(lambda k: rs(c, k).start()))
         pl.when(n == 6)(lambda: reduce_own(0))
 
     each(0, 2 * CHUNKS, phase1)
-    each(1, CHUNKS, reduce_own)
+    reduce_own(1)
+    reduce_own(2)
 
     wide = lax.broadcasted_iota(jnp.int32, (OWN // 2, 128), 1)
     glane = lax.broadcasted_iota(jnp.int32, (PROBES, 128), 1)
@@ -216,7 +244,6 @@
     gacc[...] = jnp.zeros((PROBES, 128), F32)
 
     def take_chunk(c):
-        ag_all(c).wait_recv()
         s = sfull[c]
         hi = s.astype(BF16).astype(F32)
         st[...] = jnp.transpose(jnp.concatenate([hi, s - hi], axis=0)).astype(BF16)
@@ -228,7 +255,7 @@
     def g_copy(p, r):
         return remote(
             gall.at[p, mine], gall.at[p, mine], g_s.at[p * PEERS + r], g_r.at[p * PEERS + r],
-            at_peer((mine + r) % PEERS),
+            at_peer(lax.rem(mine + r, PEERS)),
         )
 
     def send_gram(p):
@@ -236,10 +263,10 @@
         gall[p, mine] = jnp.where(
             glane[:32] < 64, v[:32], pltpu.roll(v[32:], 64, 1)
         )
-        each(1, PEERS, lambda r: g_copy(p, r).start())
+        unrolled(1, PEERS, lambda r: g_copy(p, r).start())
 
     def sum_gram(p):
-        each(1, PEERS, lambda r: g_copy(p, r).wait_recv())
+        unrolled(1, PEERS, lambda r: g_copy(p, r).wait_recv())
         v = jnp.sum(gall[p], axis=0)
         both_halves = jnp.concatenate([v, pltpu.roll(v, 64, 1)], axis=0)
         return jnp.where(glane < 64, both_halves, 0.0)
@@ -272,7 +299,7 @@
         tmat[PROBES:128, :] = jnp.where(glane >= 64, t, 0.0)
 
     def image_part(c, t):
-        yo = (y + 1 + t) % NY
+        yo = lax.rem(y + 1 + t, NY)
         return lax.dot_general(
             kmat[pl.ds(pl.multiple_of(yo * 2 * OWN, 2 * OWN), 2 * OWN), chunk_at(c)], st[...], NN,
             preferred_element_type=F32,
@@ -290,26 +317,30 @@
         zacc[t] = image_part(0, t)
 
     def one_pass(c):
+        ag_all(c).wait_recv()
         take_chunk(c)
         add_gram(c)
         each(0, NY, lambda t: add_part(c, t))
 
+    ag_all(0).wait_recv()
     take_chunk(0)
     add_gram(0)
     send_gram(0)
     each(0, NY, first_part)
+    reduce_own(3)
     each(1, CHUNKS - 1, one_pass)
     damping()
-    take_chunk(CHUNKS - 1)
+    ag_all(CHUNKS - 1).wait_recv()
     add_gram(CHUNKS - 1)
     send_gram(1)
+    take_chunk(CHUNKS - 1)
 
     def zc(t):
         return remote(zsend.at[t], zcrecv.at[t], zc_s.at[t], zc_r.at[t], at_peer(y * 2 + 1 - core))
 
     def zy(t):
         return remote(
-            zout.at[t], zyrecv.at[t], zy_s.at[t], zy_r.at[t], at_peer(((y + 1 + t) % NY) * 2 + core)
+            zout.at[t], zyrecv.at[t], zy_s.at[t], zy_r.at[t], at_peer((lax.rem(y + 1 + t, NY)) * 2 + core)
         )
 
     def last_part(t):
@@ -319,9 +350,7 @@
 
     def damped(t):
         zc(t).wait_recv()
-        return lax.dot_general(
-            merged(t, core) + zcrecv[t], tmat[...], NN, precision=HIGHEST, preferred_element_type=F32
-        )
+        return dot3(merged(t, core) + zcrecv[t], tmat[...], NN)
 
     def share(t):
         zout[t] = damped(t).astype(BF16)
@@ -331,6 +360,12 @@
     each(0, NY - 1, share)
     zmine[...] = damped(NY - 1)
 
+    own_lanes = pl.ds(pl.multiple_of((z // 2) * 128, 128), 128)
+    stile = sfull[x, :, own_lanes]
+    sown = jnp.where(z % 2 == 1, pltpu.roll(stile, 64, 1), stile)
+    sdamp = lax.dot_general(
+        tmat[0:PROBES, 0:PROBES], sown, NN, precision=HIGHEST, preferred_element_type=F32
+    )
     gram = sum_gram(1) / slab_total
     trace = jnp.sum(jnp.where(glane == grow, gram, 0.0), keepdims=True)
     m = jnp.where(glane < 64, gram, tinv[...])
@@ -352,12 +387,6 @@
     upper = jnp.where(glane >= 64, m / jnp.sqrt(d), 0.0)
     lower = pltpu.roll(upper, 64, 1)
 
-    own_lanes = pl.ds(pl.multiple_of((z // 2) * 128, 128), 128)
-    stile = sfull[x, :, own_lanes]
-    sown = jnp.where(z % 2 == 1, pltpu.roll(stile, 64, 1), stile)
-    sdamp = lax.dot_general(
-        tmat[0:PROBES, 0:PROBES], sown, NN, precision=HIGHEST, preferred_element_type=F32
-    )
     basis = lax.dot_general(
         lower[:, :PROBES], sdamp, NN, precision=HIGHEST, preferred_element_type=F32
     )
@@ -373,10 +402,9 @@
     each(0, 2, lambda p: each(1, PEERS, lambda r: g_copy(p, r).wait_send()))
     each(0, NY - 1, lambda t: zy(t).wait())
     zs = zmine[...] + (zyrecv[0].astype(F32) + zyrecv[1].astype(F32) + zyrecv[2].astype(F32))
-    for half, w in ((0, lower), (1, upper)):
-        image_ref[:, half * 512 : half * 512 + 512] = scale * lax.dot_general(
-            w, zs, NT, precision=HIGHEST, preferred_element_type=F32
-        )
+    halves = scale * dot3(jnp.concatenate([lower, upper], axis=0), zs, NT)
+    image_ref[:, : OWN // 2] = halves[:PROBES]
+    image_ref[:, OWN // 2 :] = halves[PROBES:]
 
 
 def finish_kernel(basis_in, image_in, basis_out, image_out):

time: 75.7 us -> 72.1 us (0.952)
  Pallas kernels: 74.8 us -> 71.2 us
    pallas_call x1, Pallas kernels: 73.1 us -> 69.5 us  [body(): pl.pallas_call(functools.partial(main_kernel, slab_total=A * PEERS, point...]
where the time goes in v4:
time: 72.1 us; the launch traced here: 71.8 us
  Pallas kernels  71.2 us (99%)
    pallas_call x1, Pallas kernels, body(): pl.pallas_call(functools.partial(main_kernel, slab_total=A * PEERS, point...  69.5 us
    pallas_call x1, Pallas kernels, body(): pl.pallas_call(finish_kernel, out_shape=(jax.ShapeDtypeStruct((PROBES, BL...  1.69 us

profile of v4, /device:TPU:9, one launch (start us, length us, event | category | flops | bytes accessed | tf_op | source)
XLA Modules:
  0.0 71.8 jit_solution(1056180702219703065)
XLA Ops:
  0.6 69.5 %slab_kernel.1 = (bf16[64,64]{1,0:T(8,128)(2,1)}, f32[64,1024]{1,0:T(8,128)}) custom-call(bf16[64,64]{1,0:T(8,128)(2,1)} %slab_ref.1, bf16[64,16384]{1,0:T(8,128)(2,1)} %col_ref.1, bf16[64,16384]{1,0:T(8,128)(2,1)} %probe_ref.1), custom_call_target="tpu_custom_call" | custom-call | tf_op jit(solution)/shard_map/slab_kernel/pallas_call | solution.py:419
  70.1 1.7 %finish.1 = (bf16[64,64]{1,0:T(8,128)(2,1)}, f32[64,1024]{1,0:T(8,128)}) custom-call(bf16[64,64]{1,0:T(8,128)(2,1)} %get-tuple-element.4.basis_in, f32[64,1024]{1,0:T(8,128)} %get-tuple-element.5.image_in), custom_call_target="tpu_custom_call" | custom-call | tf_op jit(solution)/shard_map/finish/pallas_call | solution.py:459

commit v5 on v4

--- a/solution.py
+++ b/solution.py
@@ -60,7 +60,7 @@
     basis_ref, image_ref,
     cols, probes, yt, xall, xaug, kmat, spart, rsrecv, sfull, st,
     zacc, zsend, zmine, zcrecv, zout, zyrecv, gacc, gall, tmat, tinv,
-    in_sem, sz_s, sz_r, sx_s, sx_r, rs_s, rs_r, ag_s, ag_r,
+    in_sem, sz_s, sz_r, sx_s, sx_r, rs_s, rs_r, az_s, az_r, ax_s, ax_r,
     zc_s, zc_r, zy_s, zy_r, g_s, g_r,
     *, slab_total, point_total,
 ):
@@ -186,10 +186,6 @@
             spart.at[(c, *there)], rsrecv.at[c, k], rs_s.at[c], rs_r.at[c], at_offset(dx, dz)
         )
 
-    def ag(c, k):
-        here = sfull.at[(c, *piece(x, z))]
-        return remote(here, here, ag_s.at[c], ag_r.at[c], at_offset(*OTHERS[k]))
-
     def to_others(f):
         for k in range(GROUP - 1):
             f(k)
@@ -197,13 +193,33 @@
     def rs_all(c):
         return remote(rsrecv.at[c], rsrecv.at[c], rs_s.at[c], rs_r.at[c], at_z(1))
 
-    def ag_all(c):
-        return remote(rsrecv.at[c], rsrecv.at[c], ag_s.at[c], ag_r.at[c], at_z(1))
-
-    def reduce_own(c):
+    def az(c, r):
+        here = sfull.at[(c, *piece(x, z))]
+        return remote(here, here, az_s.at[c], az_r.at[c], at_z(r))
+
+    def ax(c, r):
+        here = sfull.at[c, :, pl.ds(pl.multiple_of(x * 128, 128), 128)]
+        return remote(here, here, ax_s.at[c], ax_r.at[c], at_x(r))
+
+    def az_all(c):
+        some = rsrecv.at[c, pl.ds(0, NZ - 1)]
+        return remote(some, some, az_s.at[c], az_r.at[c], at_z(1))
+
+    def ax_all(c):
+        some = rsrecv.at[c, pl.ds(0, (NX - 1) * NZ)]
+        return remote(some, some, ax_s.at[c], ax_r.at[c], at_z(1))
+
+    def sum_own(c):
         rs_all(c).wait_recv()
         sfull[(c, *piece(x, z))] = spart[(c, *piece(x, z))] + jnp.sum(rsrecv[c], axis=0)
-        to_others(lambda k: ag(c, k).start())
+
+    def reduce_own(c):
+        sum_own(c)
+        unrolled(1, NZ, lambda r: az(c, r).start())
+
+    def gather_x(c):
+        az_all(c).wait_recv()
+        unrolled(1, NX, lambda r: ax(c, r).start())
 
     def chunk_at(c):
         return pl.ds(pl.multiple_of(c * CA, CA), CA)
@@ -229,14 +245,16 @@
         def _():
             slab_x((x - c + NX) % NX).wait_recv()
 
-        build_x(c)
+        pl.when((half == 0) | (c == x))(lambda: build_x(c))
         spart[c] += tile(c, half)
         pl.when(half == 1)(lambda: to_others(lambda k: rs(c, k).start()))
         pl.when(n == 6)(lambda: reduce_own(0))
 
     each(0, 2 * CHUNKS, phase1)
     reduce_own(1)
+    gather_x(0)
     reduce_own(2)
+    gather_x(1)
 
     wide = lax.broadcasted_iota(jnp.int32, (OWN // 2, 128), 1)
     glane = lax.broadcasted_iota(jnp.int32, (PROBES, 128), 1)
@@ -317,20 +335,23 @@
         zacc[t] = image_part(0, t)
 
     def one_pass(c):
-        ag_all(c).wait_recv()
+        ax_all(c).wait_recv()
         take_chunk(c)
         add_gram(c)
         each(0, NY, lambda t: add_part(c, t))
 
-    ag_all(0).wait_recv()
+    reduce_own(3)
+    gather_x(2)
+    ax_all(0).wait_recv()
     take_chunk(0)
     add_gram(0)
     send_gram(0)
     each(0, NY, first_part)
-    reduce_own(3)
-    each(1, CHUNKS - 1, one_pass)
+    one_pass(1)
+    gather_x(3)
+    one_pass(2)
     damping()
-    ag_all(CHUNKS - 1).wait_recv()
+    ax_all(CHUNKS - 1).wait_recv()
     add_gram(CHUNKS - 1)
     send_gram(1)
     take_chunk(CHUNKS - 1)
@@ -397,7 +418,8 @@
     each(1, NX, lambda r: slab_x(r).wait_send())
 
     each(0, CHUNKS, lambda c: rs_all(c).wait_send())
-    each(0, CHUNKS, lambda c: ag_all(c).wait_send())
+    each(0, CHUNKS, lambda c: az_all(c).wait_send())
+    each(0, CHUNKS, lambda c: ax_all(c).wait_send())
     each(0, NY, lambda t: zc(t).wait_send())
     each(0, 2, lambda p: each(1, PEERS, lambda r: g_copy(p, r).wait_send()))
     each(0, NY - 1, lambda t: zy(t).wait())
@@ -447,7 +469,7 @@
             pltpu.VMEM((PROBES, 128), F32),
             dma((2,)),
             dma((NZ - 1,)), dma((NZ - 1,)), dma((NX - 1,)), dma((NX - 1,)),
-            dma((CHUNKS,)), dma((CHUNKS,)), dma((CHUNKS,)), dma((CHUNKS,)),
+            dma((CHUNKS,)), dma((CHUNKS,)), dma((CHUNKS,)), dma((CHUNKS,)), dma((CHUNKS,)), dma((CHUNKS,)),
             dma((NY,)), dma((NY,)), dma((NY - 1,)), dma((NY - 1,)),
             dma((2 * PEERS,)), dma((2 * PEERS,)),
         ],

time: 72.1 us -> 70.7 us (0.981)
  Pallas kernels: 71.2 us -> 69.8 us
    pallas_call x1, Pallas kernels: 69.5 us -> 68.1 us  [body(): pl.pallas_call(functools.partial(main_kernel, slab_total=A * PEERS, point...]
where the time goes in v5:
time: 70.7 us; the launch traced here: 70.4 us
  Pallas kernels  69.8 us (99%)
    pallas_call x1, Pallas kernels, body(): pl.pallas_call(functools.partial(main_kernel, slab_total=A * PEERS, point...  68.1 us
    pallas_call x1, Pallas kernels, body(): pl.pallas_call(finish_kernel, out_shape=(jax.ShapeDtypeStruct((PROBES, BL...  1.69 us

profile of v5, /device:TPU:9, one launch (start us, length us, event | category | flops | bytes accessed | tf_op | source)
XLA Modules:
  0.0 70.4 jit_solution(3843849026293509288)
XLA Ops:
  0.6 68.1 %slab_kernel.1 = (bf16[64,64]{1,0:T(8,128)(2,1)}, f32[64,1024]{1,0:T(8,128)}) custom-call(bf16[64,64]{1,0:T(8,128)(2,1)} %slab_ref.1, bf16[64,16384]{1,0:T(8,128)(2,1)} %col_ref.1, bf16[64,16384]{1,0:T(8,128)(2,1)} %probe_ref.1), custom_call_target="tpu_custom_call" | custom-call | tf_op jit(solution)/shard_map/slab_kernel/pallas_call | solution.py:441
  68.7 1.7 %finish.1 = (bf16[64,64]{1,0:T(8,128)(2,1)}, f32[64,1024]{1,0:T(8,128)}) custom-call(bf16[64,64]{1,0:T(8,128)(2,1)} %get-tuple-element.4.basis_in, f32[64,1024]{1,0:T(8,128)} %get-tuple-element.5.image_in), custom_call_target="tpu_custom_call" | custom-call | tf_op jit(solution)/shard_map/finish/pallas_call | solution.py:481

commit v6 on v5

--- a/solution.py
+++ b/solution.py
@@ -377,8 +377,8 @@
         zout[t] = damped(t).astype(BF16)
         zy(t).start()
 
-    each(0, NY, last_part)
-    each(0, NY - 1, share)
+    unrolled(0, NY, last_part)
+    unrolled(0, NY - 1, share)
     zmine[...] = damped(NY - 1)
 
     own_lanes = pl.ds(pl.multiple_of((z // 2) * 128, 128), 128)

time: 70.7 us -> 71 us (level)
  no operation moved by 1% of the time
where the time goes in v6:
time: 71 us; the launch traced here: 70.7 us
  Pallas kernels  70.1 us (99%)
    pallas_call x1, Pallas kernels, body(): pl.pallas_call(functools.partial(main_kernel, slab_total=A * PEERS, point...  68.4 us
    pallas_call x1, Pallas kernels, body(): pl.pallas_call(finish_kernel, out_shape=(jax.ShapeDtypeStruct((PROBES, BL...  1.69 us

profile of v6, /device:TPU:9, one launch (start us, length us, event | category | flops | bytes accessed | tf_op | source)
XLA Modules:
  0.0 70.7 jit_solution(3206425640148522773)
XLA Ops:
  0.6 68.4 %slab_kernel.1 = (bf16[64,64]{1,0:T(8,128)(2,1)}, f32[64,1024]{1,0:T(8,128)}) custom-call(bf16[64,64]{1,0:T(8,128)(2,1)} %slab_ref.1, bf16[64,16384]{1,0:T(8,128)(2,1)} %col_ref.1, bf16[64,16384]{1,0:T(8,128)(2,1)} %probe_ref.1), custom_call_target="tpu_custom_call" | custom-call | tf_op jit(solution)/shard_map/slab_kernel/pallas_call | solution.py:441
  69.0 1.7 %finish.1 = (bf16[64,64]{1,0:T(8,128)(2,1)}, f32[64,1024]{1,0:T(8,128)}) custom-call(bf16[64,64]{1,0:T(8,128)(2,1)} %get-tuple-element.4.basis_in, f32[64,1024]{1,0:T(8,128)} %get-tuple-element.5.image_in), custom_call_target="tpu_custom_call" | custom-call | tf_op jit(solution)/shard_map/finish/pallas_call | solution.py:481
